TPU v7x, 1024 devices: a whole 4x4x32 slice. The times are simulated.
1024 devices in a mesh: row: 32 (over z), col: 8 (over x, core), layer: 4 (over y).
Axes of the slice: x: 4, y: 4, z: 32, core: 2. Of those that a mesh axis runs over, the one named last changes fastest.
Arguments:
- a_tiles: bfloat16 [8, 32, 4, 3, 128, 128], P('col', 'row', 'layer'), may hold values from -6 to 6
- a_occ: int32 [8, 32, 4, 3], P('col', 'row', 'layer'), may hold values from 0 to 1, as said below
- b_tiles: bfloat16 [32, 4, 32, 3, 128, 128], P('col', 'layer', 'row'), may hold values from -0.046875 to 0.046875
- b_occ: int32 [32, 4, 32, 3], P('col', 'layer', 'row'), may hold values from 0 to 1, as said below
- stacks: int32 [8, 32, 4, 32, 8, 3], P('col', 'row', 'layer'), may hold values from 0 to 3, as said below
- stack_count: int32 [8, 32, 4, 32], P('col', 'row', 'layer'), may hold values from 1 to 8, as said below
- c_keep: int32 [8, 32, 4], P('col', 'row', 'layer'), may hold values 0 or 1
Outputs:
- c_out: bfloat16 [8, 32, 4, 128, 128], P('col', 'row', 'layer')
Inputs may be any that keep to these rules, and one draw needn't show every extreme that they name: `a_occ`: 0 or 1; how full a panel is varies from panel to panel. `b_occ`: 0 or 1; how full a panel is varies from panel to panel. `stacks`: left slot s below 3 lies in row block s % 2, right slot t below 3 in column block t % 2, and the product slot is 2 * (s % 2) + (t % 2); the entries of one stack name distinct (left, right) pairs; the largest product slot occurs. `stack_count`: entries at and past the count are padding and are ignored; the largest count occurs in every draw.
All inputs are finite; a program needn't handle non-finite values. No bound on the sum of `c_keep` on one device may be relied on, other than what follows from the above.
Results may differ from a plain program's by a relative error of at most 0.001.
Values may be sent and summed in bfloat16 or wider, within the bound.
No kernel may reach another device: no remote copies, remote signals or barrier semaphores. Data moves between devices by JAX's collectives and lax.ppermute only.
A program may use at most 32 MiB of HBM per device.

v0:
```python
from functools import partial

import jax
import jax.numpy as jnp
from jax import lax
from jax.sharding import PartitionSpec as P


def pick_tiles(panels, slots):
    return jax.vmap(lambda one_panel, one_slot: one_panel[one_slot])(panels, slots)


def group_products(running, members, c_slots):
    left_group, right_group, triple_group, count_group = members
    left_sel = pick_tiles(left_group, triple_group[:, :, 0])
    right_sel = pick_tiles(right_group, triple_group[:, :, 1])
    products = jnp.einsum(
        "psij,psjk->psik", left_sel, right_sel, preferred_element_type=jnp.float32
    )
    stack_len = triple_group.shape[1]
    target = (
        triple_group[:, :, 2][:, :, None] == jnp.arange(c_slots, dtype=jnp.int32)[None, None, :]
    )
    live = jnp.arange(stack_len, dtype=jnp.int32)[None, :, None] < count_group[:, None, None]
    weights = (target & live).astype(jnp.float32)
    added = jnp.einsum("psc,psik->cik", weights, products, precision=lax.Precision.HIGHEST)
    return (running + added, None)


def panel_sum(left_panels, right_panels, triples, counts, c_slots):
    n_panels = left_panels.shape[0]
    group = max((divisor for divisor in range(1, 9) if n_panels % divisor == 0))
    steps_count = n_panels // group
    members = (
        left_panels.reshape((steps_count, group) + left_panels.shape[1:]),
        right_panels.reshape((steps_count, group) + right_panels.shape[1:]),
        triples.reshape((steps_count, group) + triples.shape[1:]),
        counts.reshape(steps_count, group),
    )
    tile_size = left_panels.shape[-1]
    initial = jnp.zeros((c_slots, tile_size, tile_size), jnp.float32)
    summed, unused = lax.scan(partial(group_products, c_slots=c_slots), initial, members)
    return summed


def local(a_tiles, a_occ, b_tiles, b_occ, stacks, stack_count, c_keep):
    c_slots = c_keep.shape[2] * lax.axis_size("layer")
    a_held = a_tiles * a_occ.astype(jnp.bfloat16)[..., None, None]
    b_held = b_tiles * b_occ.astype(jnp.bfloat16)[..., None, None]
    triples = stacks[0, 0, 0]
    counts = stack_count[0, 0, 0]
    right_all = lax.all_gather(b_held, "col", axis=0, tiled=True)
    right_all = right_all.reshape((right_all.shape[0],) + right_all.shape[3:])
    panels = lax.all_gather(a_held, "row", axis=1, tiled=True)
    n_panels = panels.shape[1]
    left_panels = panels.reshape((n_panels,) + panels.shape[3:])
    partial_sum = panel_sum(left_panels, right_all, triples, counts, c_slots)
    reduced = lax.psum_scatter(partial_sum, "layer", scatter_dimension=0, tiled=True)
    kept = reduced * c_keep[0, 0].astype(jnp.float32)[:, None, None]
    return kept.astype(jnp.bfloat16)[None, None]


def solution(mesh):
    return jax.shard_map(
        local,
        mesh=mesh,
        in_specs=(
            P("col", "row", "layer", None, None, None),
            P("col", "row", "layer", None),
            P("col", "layer", "row", None, None, None),
            P("col", "layer", "row", None),
            P("col", "row", "layer", None, None, None),
            P("col", "row", "layer", None),
            P("col", "row", "layer"),
        ),
        out_specs=P("col", "row", "layer", None, None),
        check_vma=False,
    )
```

profile of v0, /device:TPU:24, one launch (start us, length us, event | category | flops | bytes accessed | tf_op | source)
XLA Modules:
  0.0 313.2 jit_solution(16550514035073315843)
XLA Ops:
  6.5 0.7 convert_element_type.15
  7.3 1.8 broadcast_multiply_fusion
  9.2 0.7 convert_bitcast_fusion
  9.9 1.6 bitcast_multiply_fusion
  11.6 0.8 reshape_squeeze.6
  13.0 1.4 reduce.3
  14.4 48.5 %all-gather.5.cloned.1.call-done = bf16[32,1,1,3,128,128]{5,4,3,2,1,0:T(8,128)(2,1)} async-done(((bf16[4,1,1,3,128,128]{5,4,3,2,1,0:T(8,128)(2,1)}), bf16[32,1,1,3,128,128]{5,4,3,2,1,0:T(8,128)(2,1)}) %all-gather.5.cloned.1.call-update) | async-done | bytes 3145744 | tf_op jit(solution)/shard_map/all_gather | solution.py:52
  63.0 144.7 %all-gather.3.cloned.1.call-done = bf16[1,32,1,3,128,128]{5,4,3,2,0,1:T(8,128)(2,1)} async-done(((bf16[1,1,1,3,128,128]{5,4,3,2,0,1:T(8,128)(2,1)}), bf16[1,32,1,3,128,128]{5,4,3,2,0,1:T(8,128)(2,1)}) %all-gather.3.cloned.1.call-update) | async-done | bytes 3145744 | tf_op jit(solution)/shard_map/all_gather | solution.py:54
  207.6 66.9 %while.11 = (s32[]{:T(128)}, f32[4,128,128]{2,0,1:T(4,128)S(1)}, s32[4,8,8,3]{1,0,2,3:T(4,128)S(1)}, s32[4,8]{1,0:T(4,128)S(1)}, bf16[4,8,3,128,128]{4,3,2,1,0:T...) while((s32[]{:T(128)}, f32[4,128,128]{2,0,1:T(4,128)S(1)}, ...), condition=%wide.region_1.2_spmd.clone, body=%wide.region_0.1_spmd.clone.sunk | while | flops 318899648 | bytes 33037412 | solution.py:42
  207.6 1.5 dynamic-slice_bitcast_fusion.3
  209.3 2.2 gather_fusion
  211.6 2.2 gather_fusion.1
  213.7 4.2 %fusion.35 = f32[8,8,128,128]{3,2,1,0:T(8,128)} fusion(bf16[8,8,128,128]{3,2,1,0:T(8,128)(2,1)S(1)} %bitcast.59, bf16[8,8,128,128]{3,2,1,0:T(8,128)(2,1)} %bitcast.60), kind=kOutput, calls=%fused_computation.32.clone.1 | convolution fusion | flops 268435456 | bytes 8388608 | tf_op jit(solution)/shard_map/while/body/eval_jaxpr/psij,psjk->psik/dot_general | solution.py:17
  218.0 6.3 %fusion.37 = f32[4,128,128]{2,0,1:T(4,128)S(1)} fusion(f32[8,8,128,128]{3,2,1,0:T(8,128)} %fusion.35, f32[4,128,128]{2,0,1:T(4,128)S(1)} %get-tuple-element.144, pred[]{:T(512)S(6)} %compare.3, s32[8,8]{1,0:T(8,128)S(1)} %get-tuple-element.134, pred[8,8]{1,0:T(8,128)(4,1)S(1)} %iota_compare_fusion.3), kind=kOutput, calls=%fused_computation.5.clone.1 | convolution fusion | flops 50463232 | bytes 4718913 | tf_op jit(solution)/shard_map/while/body/eval_jaxpr/psc,psik->cik/dot_general | solution.py:26
  224.3 1.5 dynamic-slice_bitcast_fusion.3
  226.0 2.2 gather_fusion
  228.3 2.2 gather_fusion.1
  230.4 4.2 %fusion.35 = f32[8,8,128,128]{3,2,1,0:T(8,128)} fusion(bf16[8,8,128,128]{3,2,1,0:T(8,128)(2,1)S(1)} %bitcast.59, bf16[8,8,128,128]{3,2,1,0:T(8,128)(2,1)} %bitcast.60), kind=kOutput, calls=%fused_computation.32.clone.1 | convolution fusion | flops 268435456 | bytes 8388608 | tf_op jit(solution)/shard_map/while/body/eval_jaxpr/psij,psjk->psik/dot_general | solution.py:17
  234.7 6.3 %fusion.37 = f32[4,128,128]{2,0,1:T(4,128)S(1)} fusion(f32[8,8,128,128]{3,2,1,0:T(8,128)} %fusion.35, f32[4,128,128]{2,0,1:T(4,128)S(1)} %get-tuple-element.144, pred[]{:T(512)S(6)} %compare.3, s32[8,8]{1,0:T(8,128)S(1)} %get-tuple-element.134, pred[8,8]{1,0:T(8,128)(4,1)S(1)} %iota_compare_fusion.3), kind=kOutput, calls=%fused_computation.5.clone.1 | convolution fusion | flops 50463232 | bytes 4718913 | tf_op jit(solution)/shard_map/while/body/eval_jaxpr/psc,psik->cik/dot_general | solution.py:26
  241.1 1.5 dynamic-slice_bitcast_fusion.3
  242.7 2.2 gather_fusion
  245.0 2.2 gather_fusion.1
  247.2 4.2 %fusion.35 = f32[8,8,128,128]{3,2,1,0:T(8,128)} fusion(bf16[8,8,128,128]{3,2,1,0:T(8,128)(2,1)S(1)} %bitcast.59, bf16[8,8,128,128]{3,2,1,0:T(8,128)(2,1)} %bitcast.60), kind=kOutput, calls=%fused_computation.32.clone.1 | convolution fusion | flops 268435456 | bytes 8388608 | tf_op jit(solution)/shard_map/while/body/eval_jaxpr/psij,psjk->psik/dot_general | solution.py:17
  251.5 6.3 %fusion.37 = f32[4,128,128]{2,0,1:T(4,128)S(1)} fusion(f32[8,8,128,128]{3,2,1,0:T(8,128)} %fusion.35, f32[4,128,128]{2,0,1:T(4,128)S(1)} %get-tuple-element.144, pred[]{:T(512)S(6)} %compare.3, s32[8,8]{1,0:T(8,128)S(1)} %get-tuple-element.134, pred[8,8]{1,0:T(8,128)(4,1)S(1)} %iota_compare_fusion.3), kind=kOutput, calls=%fused_computation.5.clone.1 | convolution fusion | flops 50463232 | bytes 4718913 | tf_op jit(solution)/shard_map/while/body/eval_jaxpr/psc,psik->cik/dot_general | solution.py:26
  257.8 1.5 dynamic-slice_bitcast_fusion.3
  259.5 2.2 gather_fusion
  261.7 2.2 gather_fusion.1
  263.9 4.2 %fusion.35 = f32[8,8,128,128]{3,2,1,0:T(8,128)} fusion(bf16[8,8,128,128]{3,2,1,0:T(8,128)(2,1)S(1)} %bitcast.59, bf16[8,8,128,128]{3,2,1,0:T(8,128)(2,1)} %bitcast.60), kind=kOutput, calls=%fused_computation.32.clone.1 | convolution fusion | flops 268435456 | bytes 8388608 | tf_op jit(solution)/shard_map/while/body/eval_jaxpr/psij,psjk->psik/dot_general | solution.py:17
  268.2 6.3 %fusion.37 = f32[4,128,128]{2,0,1:T(4,128)S(1)} fusion(f32[8,8,128,128]{3,2,1,0:T(8,128)} %fusion.35, f32[4,128,128]{2,0,1:T(4,128)S(1)} %get-tuple-element.144, pred[]{:T(512)S(6)} %compare.3, s32[8,8]{1,0:T(8,128)S(1)} %get-tuple-element.134, pred[8,8]{1,0:T(8,128)(4,1)S(1)} %iota_compare_fusion.3), kind=kOutput, calls=%fused_computation.5.clone.1 | convolution fusion | flops 50463232 | bytes 4718913 | tf_op jit(solution)/shard_map/while/body/eval_jaxpr/psc,psik->cik/dot_general | solution.py:26
  274.5 0.7 copy.17
  275.9 29.3 %reduce-scatter.2.cloned.1.call-done = f32[1,128,128]{2,1,0:T(8,128)} async-done(((f32[4,128,128]{2,1,0:T(8,128)}), f32[1,128,128]{2,1,0:T(8,128)}) %reduce-scatter.2.cloned.1.call-update) | async-done | bytes 65552 | tf_op jit(solution)/shard_map/reduce_scatter | solution.py:58
  305.2 1.5 fusion.20
  (46 shorter events, 2.3 us)
Async XLA Ops:
  6.5 56.4 %all-gather.5.cloned.1.call-start = ((), (), s32[]{:S(2)}) async-start(), calls=%async_computation.2 | async-start | bytes 3538944 | tf_op jit(solution)/shard_map/all_gather | solution.py:52
  9.2 198.4 %all-gather.3.cloned.1.call-start = ((), (), s32[]{:S(2)}) async-start(), calls=%async_computation.1 | async-start | bytes 3244032 | tf_op jit(solution)/shard_map/all_gather | solution.py:54
  11.5 293.7 %reduce-scatter.2.cloned.1.call-start = ((), (), s32[]{:S(2)}) async-start(), calls=%async_computation.3 | async-start | bytes 327680 | tf_op jit(solution)/shard_map/reduce_scatter | solution.py:58
  211.6 2.2 copy-start
  228.3 2.2 copy-start
  245.0 2.2 copy-start
  261.7 2.2 copy-start
Sparse Core Ops, SparseCore 0:
  10.1 52.8 all-gather.4
  65.6 141.9 all-gather.2
  275.4 29.7 reduce-scatter.1
where the time goes:
time: 314 us; the launch traced here: 313 us
  waiting for transfers between devices  223 us (71%)
  matrix products  42.1 us (13%)
  local copies, waits for them, and re-layouts  26.5 us (8%)
  between operations  13.8 us (4%)
  other arithmetic  7.95 us (3%)
    all_gather x1, waiting for transfers between devices, local(): panels = lax.all_gather(a_held, 'row', axis=1, tiled=True)  145 us
    all_gather x1, waiting for transfers between devices, local(): right_all = lax.all_gather(b_held, 'col', axis=0, tiled=True)  48.5 us
    reduce_scatter x1, waiting for transfers between devices, local(): lax.psum_scatter(partial_sum, 'layer', scatter_dimension=0, tiled=True)  29.3 us
    dot_general x4, matrix products, group_products(): jnp.einsum('psc,psik->cik', weights, products, precision=lax.Precision.HI...  25.2 us
    gather x16, local copies, waits for them, and re-layouts, pick_tiles(): one_panel[one_slot]  18 us
    dot_general x4, matrix products, group_products(): jnp.einsum('psij,psjk->psik', left_sel, right_sel, preferred_element_type...  16.9 us
  transfers between devices with their start and end apart: 3, of which 3 were waited for; matrix products, arithmetic and copies ran while one was open for 2% of the time, Pallas kernels for 0%

commit v1 on v0

v1 whole, which is shorter than its diff:
```python
import jax
import jax.numpy as jnp
from jax import lax
from jax.experimental import pallas as pl
from jax.experimental.pallas import tpu as pltpu
from jax.sharding import Mesh, PartitionSpec as P

TILE = 128
LEFT = 3
RIGHT = 3
PANEL = LEFT * TILE
W_ROWS = 16


def encode(values):
    size = jnp.abs(values)
    least = 2.0**-126
    exponent = jnp.floor(jnp.log(jnp.maximum(size, least)) * 1.4426950408889634)
    exponent = jnp.maximum(exponent, -126.0)
    scaled = size * jnp.exp2(-exponent)
    code = jnp.floor((exponent + 126.0 + scaled) * 128.0 + 0.5)
    code = jnp.where(size < least, 0.0, code)
    return jnp.where(values < 0, -code, code).astype(jnp.int32).astype(jnp.int16)


def decode(codes):
    wide = codes.astype(jnp.int32)
    size = jnp.abs(wide)
    power = jnp.exp2(((size >> 7) - 127).astype(jnp.float32))
    value = (1.0 + (size & 127).astype(jnp.float32) * (1.0 / 128.0)) * power
    value = jnp.where(size < 128, 0.0, value)
    return jnp.where(wide < 0, -value, value).astype(jnp.bfloat16)


def prepare(a_ref, a_occ, b_ref, b_occ, stacks, counts, code_ref, send_ref, w_scr):
    for s in range(LEFT):
        held = a_ref[s].astype(jnp.float32) * a_occ[0, 0, 0, s].astype(jnp.float32)
        code_ref[s] = encode(held)
    for panel in range(4):
        for t in range(RIGHT):
            bit = b_occ[panel, 0, 0, t]
            row = (panel // 2) * PANEL + t * TILE
            tile = b_ref[panel, t]
            send_ref[panel % 2, row : row + TILE] = jnp.where(bit > 0, tile, jnp.zeros_like(tile))
    lanes = lax.broadcasted_iota(jnp.int32, (8, TILE), 1)
    entries = lax.broadcasted_iota(jnp.int32, (8, TILE), 0)
    for k in range(32):
        triple = stacks[k]
        pair = triple[:, 0:1] * RIGHT + triple[:, 1:2]
        hit = (jnp.broadcast_to(pair, (8, TILE)) == lanes) & (entries < counts[0, 0, 0, k])
        w_scr[k % 2, k // 2] = jnp.sum(jnp.where(hit, 1.0, 0.0), axis=0)
    send_ref[:, 2 * PANEL :] = w_scr[...].astype(jnp.bfloat16)


def products(code_ref, b_ref, w_ref, out_ref, w_scr):
    step = pl.program_id(0)

    @pl.when(step == 0)
    def _():
        out_ref[...] = jnp.zeros_like(out_ref)
        w_scr[...] = w_ref[...].astype(jnp.float32)

    def weighted(at, q, s, t):
        row = w_scr[q, pl.ds(2 * step + at, 1), :]
        weight = jnp.broadcast_to(row[:, s * RIGHT + t : s * RIGHT + t + 1], (16, TILE)).astype(jnp.bfloat16)
        tile = b_ref[0, q, at * PANEL + t * TILE : at * PANEL + (t + 1) * TILE]
        return (tile.reshape(8, 16, TILE) * weight[None]).reshape(TILE, TILE)

    left = [[decode(code_ref[at, s]) for s in range(LEFT)] for at in range(2)]
    for block, members in ((0, (0, 2)), (1, (1,))):
        lhs = jnp.concatenate([left[at][s] for at in range(2) for s in members], axis=1)
        extra = []
        for q in range(2):
            rhs = jnp.concatenate(
                [
                    jnp.concatenate([weighted(at, q, s, 0), weighted(at, q, s, 1)], axis=1)
                    for at in range(2)
                    for s in members
                ],
                axis=0,
            )
            both = jnp.dot(lhs, rhs, preferred_element_type=jnp.float32)
            out_ref[2 * block, q] += both[:, :TILE]
            out_ref[2 * block + 1, q] += both[:, TILE:]
            extra.append(
                jnp.concatenate([weighted(at, q, s, 2) for at in range(2) for s in members], axis=0)
            )
        both = jnp.dot(lhs, jnp.concatenate(extra, axis=1), preferred_element_type=jnp.float32)
        out_ref[2 * block, 0] += both[:, :TILE]
        out_ref[2 * block, 1] += both[:, TILE:]


def local(a_tiles, a_occ, b_tiles, b_occ, stacks, stack_count, c_keep):
    vmem = pl.BlockSpec(memory_space=pltpu.VMEM)
    smem = pl.BlockSpec(memory_space=pltpu.SMEM)
    codes, send = pl.pallas_call(
        prepare,
        out_shape=(
            jax.ShapeDtypeStruct((LEFT, TILE, TILE), jnp.int16),
            jax.ShapeDtypeStruct((2, 2 * PANEL + W_ROWS, TILE), jnp.bfloat16),
        ),
        in_specs=[vmem, smem, vmem, smem, vmem, smem],
        out_specs=(vmem, vmem),
        scratch_shapes=[pltpu.VMEM((2, W_ROWS, TILE), jnp.float32)],
        name="prepare",
    )(a_tiles[0, 0, 0], a_occ, b_tiles[:, 0, 0], b_occ, stacks[0, 0, 0], stack_count)
    pair = lax.all_to_all(send, "row_low", 0, 0, tiled=True)
    right_all = lax.all_gather(pair, "col", axis=0)
    left_all = lax.all_gather(codes, "row_high", axis=0)
    n_cols = right_all.shape[0]
    partial = pl.pallas_call(
        products,
        grid=(n_cols,),
        out_shape=jax.ShapeDtypeStruct((4, 2, TILE, TILE), jnp.float32),
        in_specs=[
            pl.BlockSpec((2, LEFT, TILE, TILE), lambda g: (g, 0, 0, 0)),
            pl.BlockSpec((1, 2, 2 * PANEL, TILE), lambda g: (g, 0, 0, 0)),
            pl.BlockSpec((2, W_ROWS, TILE), lambda g: (0, 2 * PANEL // W_ROWS, 0)),
        ],
        out_specs=pl.BlockSpec((4, 2, TILE, TILE), lambda g: (0, 0, 0, 0)),
        scratch_shapes=[pltpu.VMEM((2, W_ROWS, TILE), jnp.float32)],
        compiler_params=pltpu.CompilerParams(vmem_limit_bytes=24 * 1024 * 1024),
        name="products",
    )(left_all, right_all, pair)
    shares = lax.all_to_all(
        partial.reshape(8, TILE, TILE), ("layer", "row_low"), 0, 0, tiled=True
    )
    kept = jnp.sum(shares, axis=0) * c_keep[0, 0, 0].astype(jnp.float32)
    return kept.astype(jnp.bfloat16)[None, None, None]


def solution(mesh):
    rows, cols, layers = (mesh.shape[name] for name in ("row", "col", "layer"))
    paired = Mesh(
        mesh.devices.reshape(rows // 2, 2, cols, layers), ("row_high", "row_low", "col", "layer")
    )
    row = ("row_high", "row_low")
    return jax.shard_map(
        local,
        mesh=paired,
        in_specs=(
            P("col", row, "layer", None, None, None),
            P("col", row, "layer", None),
            P("col", "layer", row, None, None, None),
            P("col", "layer", row, None),
            P("col", row, "layer", None, None, None),
            P("col", row, "layer", None),
            P("col", row, "layer"),
        ),
        out_specs=P("col", row, "layer", None, None),
        check_vma=False,
    )
```

time: 314 us -> 125 us (0.40)
  the two profiles are of different devices: /device:TPU:24 before, /device:TPU:2 now
where the time goes in v1:
time: 125 us; the launch traced here: 124 us
  blocking collectives  83 us (66%)
  between operations  14.1 us (11%)
  Pallas kernels  8.3 us (7%)
  waiting for transfers between devices  8.05 us (6%)
  local copies, waits for them, and re-layouts  5.72 us (5%)
  starting transfers between devices  4.47 us (4%)
    all_gather x1, blocking collectives, local(): left_all = lax.all_gather(codes, 'row_high', axis=0)  71.6 us
    all_to_all x1, blocking collectives, local(): pair = lax.all_to_all(send, 'row_low', 0, 0, tiled=True)  11.4 us
    all_to_all x1, waiting for transfers between devices, local(): lax.all_to_all(partial.reshape(8, TILE, TILE), ('layer', 'row_low'), 0, 0...  8.04 us
    pallas_call x1, Pallas kernels, local(): pl.pallas_call(products, grid=(n_cols,), out_shape=jax.ShapeDtypeStruct((...  6.08 us
    unnamed x6, local copies, waits for them, and re-layouts  5.72 us
    all_to_all x1, starting transfers between devices, local(): lax.all_to_all(partial.reshape(8, TILE, TILE), ('layer', 'row_low'), 0, 0...  4.47 us
  transfers between devices with their start and end apart: 2, of which 1 were waited for; matrix products, arithmetic and copies ran while one was open for 0% of the time, Pallas kernels for 0%

profile of v1, /device:TPU:2, one launch (start us, length us, event | category | flops | bytes accessed | tf_op | source)
XLA Modules:
  0.0 124.2 jit_solution(5702451506953571006)
XLA Ops:
  6.5 0.0 all-gather.5.cloned.1.call-start
  6.5 1.5 %copy.10 = s32[1,1,1,32,8,3]{5,4,3,2,1,0:T(8,128)} copy(s32[1,1,1,32,8,3]{3,4,5,2,1,0:T(8,128)} %param.11) | data formatting | bytes 6144 | tf_op args[4]
  8.0 1.3 %copy.11.b_occ = s32[4,1,1,3]{3,2,1,0:T(1,128)} copy(s32[4,1,1,3]{0,2,3,1:T(1,128)} %param.10) | data formatting | bytes 96 | tf_op args[3]
  9.4 2.2 %prepare.1 = (s16[3,128,128]{2,1,0:T(8,128)(2,1)}, bf16[2,784,128]{2,1,0:T(8,128)(2,1)}) custom-call(bf16[3,128,128]{2,1,0:T(8,128)(2,1)} %bitcast.13, s32[1,1,1,3]{3,2,1,0:T(1,128)} %a_occ.1, bf16[4,3,128,128]{3,2,1,0:T(8,128)(2,1)} %bitcast.12, s32[4,1,1,3]{3,2,1,0:T(1,128)} %copy.11.b_occ, s32[32,8,3]{2,1,0:T(8,128)} %bitcast.11, s32[1,1,1,32]{3,2,1,0:T(1,128)} %counts.1), custom_call_target="tpu_custom_call" | custom-call | tf_op jit(solution)/shard_map/prepare/pallas_call | solution.py:96
  11.6 11.4 %all_to_all.10.w_ref = bf16[2,784,128]{2,1,0:T(8,128)(2,1)} all-to-all(bf16[2,784,128]{2,1,0:T(8,128)(2,1)} %get-tuple-element.8), channel_id=1, replica_groups=mesh['row_high'=16,'row_low'=2,'col'=8,'layer'=4] {'row_low'}, dimensions={0} | all-to-all | bytes 802816 | tf_op jit(solution)/shard_map/all_to_all | solution.py:107
  23.0 0.0 all-gather.5.cloned.1.call-update
  23.0 71.6 %all-gather.6 = s16[48,128,128]{2,1,0:T(8,128)(2,1)S(1)} all-gather(s16[3,128,128]{2,1,0:T(8,128)(2,1)} %get-tuple-element.7), channel_id=2, replica_groups=mesh['row_high'=16,'row_low'=2,'col'=8,'layer'=4] {'row_high'}, dimensions={0}, use_global_device_ids=true | all-gather | bytes 1671168 | tf_op jit(solution)/shard_map/all_gather | solution.py:109
  94.6 0.0 all-gather.5.cloned.1.call-done
  94.6 0.0 copy-start
  94.6 1.0 copy-done
  95.6 0.0 copy-start.1
  95.6 1.9 %copy-done.1 = bf16[16,784,128]{2,1,0:T(8,128)(2,1)S(1)} copy-done((bf16[16,784,128]{2,1,0:T(8,128)(2,1)S(1)}, bf16[16,784,128]{2,1,0:T(8,128)(2,1)}, u32[]{:S(2)}) %copy-start.1) | copy-done | bytes 3211288
  97.5 6.1 %products.1 = f32[4,2,128,128]{3,2,1,0:T(8,128)} custom-call(s16[16,3,128,128]{3,2,1,0:T(8,128)(2,1)S(1)} %bitcast.9, bf16[8,2,784,128]{3,2,1,0:T(8,128)(2,1)S(1)} %bitcast.10, bf16[2,784,128]{2,1,0:T(8,128)(2,1)S(1)} %copy-done), custom_call_target="tpu_custom_call" | custom-call | tf_op jit(solution)/shard_map/products/pallas_call | solution.py:111
  103.6 4.5 %all-to-all-start.1 = ((f32[8,128,128]{2,1,0:T(8,128)}), f32[8,128,128]{2,1,0:T(8,128)S(1)}, u32[]{:S(2)}, u32[]{:S(2)}) async-start(f32[8,128,128]{2,1,0:T(8,128)} %bitcast.5), calls=%async_computation.1 | async-start | bytes 1048576 | tf_op jit(solution)/shard_map/all_to_all | solution.py:125
  108.7 8.0 %all-to-all-done.1 = f32[8,128,128]{2,1,0:T(8,128)S(1)} async-done(((f32[8,128,128]{2,1,0:T(8,128)}), f32[8,128,128]{2,1,0:T(8,128)S(1)}, u32[]{:S(2)}, u32[]{:S(2)}) %all-to-all-start.1) | async-done | bytes 524320 | tf_op jit(solution)/shard_map/all_to_all | solution.py:125
  116.8 0.6 fusion
  (1 shorter events, 0.0 us)
Async XLA Ops:
  6.5 88.0 %all-gather.5.cloned.1.call-start = ((), (), s32[]{:S(2)}) async-start(), calls=%async_computation.2 | async-start | bytes 3612672 | tf_op jit(solution)/shard_map/all_gather | solution.py:108
  94.6 1.0 copy-start
  95.6 1.9 %copy-start.1 = (bf16[16,784,128]{2,1,0:T(8,128)(2,1)S(1)}, bf16[16,784,128]{2,1,0:T(8,128)(2,1)}, u32[]{:S(2)}) copy-start(bf16[16,784,128]{2,1,0:T(8,128)(2,1)} %all-gather.5.cloned.1.call-done) | copy-start | bytes 9633796
  103.6 13.2 %all-to-all-start.1 = ((f32[8,128,128]{2,1,0:T(8,128)}), f32[8,128,128]{2,1,0:T(8,128)S(1)}, u32[]{:S(2)}, u32[]{:S(2)}) async-start(f32[8,128,128]{2,1,0:T(8,128)} %bitcast.5), calls=%async_computation.1 | async-start | bytes 1048576 | tf_op jit(solution)/shard_map/all_to_all | solution.py:125
Sparse Core Ops, SparseCore 0:
  23.1 52.4 all-gather.4

commit v2 on v1

v2 whole, which is shorter than its diff:
```python
import jax
import jax.numpy as jnp
from jax import lax
from jax.experimental import pallas as pl
from jax.experimental.pallas import tpu as pltpu
from jax.sharding import Mesh, PartitionSpec as P

TILE = 128
LEFT = 3
RIGHT = 3
PANEL = LEFT * TILE
W_ROWS = 16
BLOCK = 2 * PANEL + W_ROWS


def encode(values):
    size = jnp.abs(values)
    least = 2.0**-124
    exponent = jnp.floor(jnp.log(jnp.maximum(size, least)) * 1.4426950408889634)
    scaled = size * jnp.exp2(-exponent)
    exponent = jnp.where(scaled >= 1.996, exponent + 1.0, jnp.where(scaled < 0.998, exponent - 1.0, exponent))
    exponent = jnp.maximum(exponent, -124.0)
    significand = jnp.floor(size * jnp.exp2(-exponent) * 128.0 + 0.5)
    significand = jnp.where(values < 0, -significand, significand)
    code = jnp.where(size < least, 0.0, (exponent + 61.0) * 512.0 + significand)
    return code.astype(jnp.int32).astype(jnp.int16)


def decode(codes):
    scaled = codes.astype(jnp.int32).astype(jnp.float32) * (1.0 / 128.0)
    exponent = jnp.floor(scaled * 0.25 + 0.5)
    return ((scaled - 4.0 * exponent) * jnp.exp2(exponent - 61.0)).astype(jnp.bfloat16)


def right_block(low, parity, b_ref, b_occ, block):
    for half in range(2):
        for t in range(RIGHT):
            row = half * PANEL + t * TILE
            panel = 2 * half + parity
            tile = b_ref[panel, t]
            block[row : row + TILE] = jnp.where(b_occ[0, t, 0, panel] > 0, tile, jnp.zeros_like(tile))


def stack_weights(stacks, counts):
    pair = stacks[0] * RIGHT + stacks[1]
    live = lax.broadcasted_iota(jnp.int32, pair.shape, 0) < counts[0, 0]
    rows = lax.broadcasted_iota(jnp.int32, (W_ROWS, pair.shape[1]), 0)
    weights = jnp.zeros(rows.shape, jnp.float32)
    for number in range(LEFT * RIGHT):
        used = jnp.where(live & (pair == number), 1.0, 0.0)
        weights = jnp.where(rows == number, jnp.sum(used, axis=0, keepdims=True), weights)
    return jnp.concatenate([weights] * (TILE // pair.shape[1]), axis=1)


def put_weights(parity, weights, block):
    shifted = jnp.concatenate([weights[:, 1:], weights[:, :1]], axis=1)
    block[2 * PANEL :] = jnp.where(parity == 0, weights, shifted).astype(jnp.bfloat16)


def copy_all(source, out_ref, slot, sems):
    copies = [
        pltpu.make_async_copy(source, out_ref.at[at, slot], sems.at[at]) for at in range(out_ref.shape[0])
    ]
    for copy in copies:
        copy.start()
    return copies


def prepare_other(low_ref, b_ref, b_occ, stacks, counts, send_ref):
    low = low_ref[0]
    put_weights(1 - low, stack_weights(stacks, counts), send_ref)
    right_block(low, 1 - low, b_ref, b_occ, send_ref)


def prepare_own(low_ref, b_ref, b_occ, stacks, counts, a_ref, a_occ, out_ref, code_ref, own, sems):
    low = low_ref[0]
    put_weights(low, stack_weights(stacks, counts), own)
    right_block(low, low, b_ref, b_occ, own)
    copies = copy_all(own, out_ref, low, sems)
    for s in range(LEFT):
        held = a_ref[s].astype(jnp.float32) * a_occ[0, 0, 0, s].astype(jnp.float32)
        code_ref[0, s * TILE : (s + 1) * TILE] = encode(held)
    for copy in copies:
        copy.wait()


def add_other(low_ref, other, _, out_ref, sems):
    for copy in copy_all(other, out_ref, 1 - low_ref[0], sems):
        copy.wait()


def products(col_ref, code_ref, b_ref, out_ref):
    n_cols = b_ref.shape[0]
    out_ref[...] = jnp.zeros_like(out_ref)
    lanes = lax.broadcasted_iota(jnp.int32, (W_ROWS, TILE), 1)
    weights = [b_ref[col_ref[0], q, 2 * PANEL :].astype(jnp.float32) for q in range(2)]

    for g in range(n_cols):
        chosen = [
            [
                jnp.sum(jnp.where(lanes == 2 * (2 * g + at), weights[q], 0.0), axis=1, keepdims=True)
                for q in range(2)
            ]
            for at in range(2)
        ]

        def weighted(at, q, s, t):
            number = s * RIGHT + t
            weight = jnp.broadcast_to(chosen[at][q][number : number + 1], (16, TILE)).astype(jnp.bfloat16)
            row = at * PANEL + t * TILE
            tile = b_ref[g, q, row : row + TILE]
            return (tile.reshape(8, 16, TILE) * weight[None]).reshape(TILE, TILE)

        left = [
            [decode(code_ref[2 * g + at, s * TILE : (s + 1) * TILE]) for s in range(LEFT)]
            for at in range(2)
        ]
        for block, members in ((0, (0, 2)), (1, (1,))):
            lhs = jnp.concatenate([left[at][s] for at in range(2) for s in members], axis=1)
            extra = []
            for q in range(2):
                rhs = jnp.concatenate(
                    [
                        jnp.concatenate([weighted(at, q, s, 0), weighted(at, q, s, 1)], axis=1)
                        for at in range(2)
                        for s in members
                    ],
                    axis=0,
                )
                both = jnp.dot(lhs, rhs, preferred_element_type=jnp.float32)
                out_ref[2 * block, q] += both[:, :TILE]
                out_ref[2 * block + 1, q] += both[:, TILE:]
                extra.append(
                    jnp.concatenate([weighted(at, q, s, 2) for at in range(2) for s in members], axis=0)
                )
            both = jnp.dot(lhs, jnp.concatenate(extra, axis=1), preferred_element_type=jnp.float32)
            out_ref[2 * block, 0] += both[:, :TILE]
            out_ref[2 * block, 1] += both[:, TILE:]


def local(a_tiles, a_occ, b_tiles, b_occ, stacks, stack_count, c_keep):
    n_cols = lax.axis_size("col")
    vmem = pl.BlockSpec(memory_space=pltpu.VMEM)
    smem = pl.BlockSpec(memory_space=pltpu.SMEM)
    hbm = pl.BlockSpec(memory_space=pltpu.HBM)
    low = lax.axis_index("row_low").reshape(1)
    spread = jax.ShapeDtypeStruct((n_cols, 2, BLOCK, TILE), jnp.bfloat16)
    right_args = (
        b_tiles[:, 0, 0],
        b_occ.transpose(1, 3, 2, 0),
        stacks[0, 0, 0].transpose(2, 1, 0),
        stack_count,
    )
    send = pl.pallas_call(
        prepare_other,
        out_shape=jax.ShapeDtypeStruct((BLOCK, TILE), jnp.bfloat16),
        in_specs=[smem, vmem, smem, vmem, vmem],
        out_specs=vmem,
        name="prepare_other",
    )(low, *right_args)
    other = lax.ppermute(send, "row_low", [(0, 1), (1, 0)])
    right, codes = pl.pallas_call(
        prepare_own,
        out_shape=(spread, jax.ShapeDtypeStruct((1, PANEL, TILE), jnp.int16)),
        in_specs=[smem, vmem, smem, vmem, vmem, vmem, smem],
        out_specs=(hbm, vmem),
        scratch_shapes=[pltpu.VMEM((BLOCK, TILE), jnp.bfloat16), pltpu.SemaphoreType.DMA((n_cols,))],
        cost_estimate=pl.CostEstimate(flops=10_000_000, bytes_accessed=4_000_000, transcendentals=0),
        name="prepare_own",
    )(low, *right_args, a_tiles[0, 0, 0], a_occ)
    other, right, codes = lax.optimization_barrier((other, right, codes))
    right = pl.pallas_call(
        add_other,
        out_shape=spread,
        in_specs=[smem, vmem, hbm],
        out_specs=hbm,
        scratch_shapes=[pltpu.SemaphoreType.DMA((n_cols,))],
        input_output_aliases={2: 0},
        compiler_params=pltpu.CompilerParams(vmem_limit_bytes=54_000_000),
        name="add_other",
    )(low, other, right)
    right_all = lax.all_to_all(right, "col", 0, 0, tiled=True)
    left_all = lax.all_gather(codes, "row_high", axis=0, tiled=True)
    partial = pl.pallas_call(
        products,
        out_shape=jax.ShapeDtypeStruct((4, 2, TILE, TILE), jnp.float32),
        in_specs=[smem, vmem, vmem],
        out_specs=vmem,
        compiler_params=pltpu.CompilerParams(vmem_limit_bytes=16 * 1024 * 1024),
        name="products",
    )(lax.axis_index("col").reshape(1), left_all, right_all)
    shares = lax.all_to_all(
        partial.reshape(8, TILE, TILE), ("layer", "row_low"), 0, 0, tiled=True
    )
    kept = jnp.sum(shares, axis=0) * c_keep[0, 0, 0].astype(jnp.float32)
    return kept.astype(jnp.bfloat16)[None, None, None]


def solution(mesh):
    rows, cols, layers = (mesh.shape[name] for name in ("row", "col", "layer"))
    paired = Mesh(
        mesh.devices.reshape(rows // 2, 2, cols, layers), ("row_high", "row_low", "col", "layer")
    )
    row = ("row_high", "row_low")
    return jax.shard_map(
        local,
        mesh=paired,
        in_specs=(
            P("col", row, "layer", None, None, None),
            P("col", row, "layer", None),
            P("col", "layer", row, None, None, None),
            P("col", "layer", row, None),
            P("col", row, "layer", None, None, None),
            P("col", row, "layer", None),
            P("col", row, "layer"),
        ),
        out_specs=P("col", row, "layer", None, None),
        check_vma=False,
    )
```

time: 125 us -> 110 us (0.88)
  the two profiles are of different devices: /device:TPU:2 before, /device:TPU:24 now
where the time goes in v2:
time: 110 us; the launch traced here: 109 us
  blocking collectives  75.4 us (69%)
  starting transfers between devices  12.9 us (12%)
  Pallas kernels  9.02 us (8%)
  waiting for transfers between devices  7.7 us (7%)
  local copies, waits for them, and re-layouts  2.2 us (2%)
    all_gather x1, blocking collectives, local(): left_all = lax.all_gather(codes, 'row_high', axis=0, tiled=True)  75.4 us
    all_to_all x1, waiting for transfers between devices, local(): lax.all_to_all(partial.reshape(8, TILE, TILE), ('layer', 'row_low'), 0, 0...  5.66 us
    all_to_all x1, starting transfers between devices, local(): lax.all_to_all(partial.reshape(8, TILE, TILE), ('layer', 'row_low'), 0, 0...  4.69 us
    all_to_all x1, starting transfers between devices, local(): right_all = lax.all_to_all(right, 'col', 0, 0, tiled=True)  4.44 us
    ppermute x1, starting transfers between devices, local(): other = lax.ppermute(send, 'row_low', [(0, 1), (1, 0)])  3.81 us
    pallas_call x1, Pallas kernels, local(): pl.pallas_call(prepare_own, out_shape=(spread, jax.ShapeDtypeStruct((1, P...  3.13 us
    pallas_call x1, Pallas kernels, local(): pl.pallas_call(products, out_shape=jax.ShapeDtypeStruct((4, 2, TILE, TILE...  2.77 us
  transfers between devices with their start and end apart: 3, of which 2 were waited for; matrix products, arithmetic and copies ran while one was open for 0% of the time, Pallas kernels for 3%

profile of v2, /device:TPU:24, one launch (start us, length us, event | category | flops | bytes accessed | tf_op | source)
XLA Modules:
  0.0 108.7 jit_solution(4972593299364265646)
XLA Ops:
  0.0 1.9 %prepare_other.1 = bf16[784,128]{1,0:T(8,128)(2,1)} custom-call(s32[1]{0:T(128)} %bitcast.1.low_ref, bf16[4,3,128,128]{3,2,1,0:T(8,128)(2,1)} %bitcast.13, s32[1,3,1,4]{3,2,1,0:T(1,128)} %bitcast.18, s32[3,8,32]{2,1,0:T(8,128)} %bitcast.16, s32[1,1,1,32]{3,2,1,0:T(1,128)} %counts.3), custom_call_target="tpu_custom_call" | custom-call | tf_op jit(solution)/shard_map/prepare_other/pallas_call | solution.py:154
  1.9 3.8 %collective-permute-start = (bf16[784,128]{1,0:T(8,128)(2,1)}, bf16[784,128]{1,0:T(8,128)(2,1)S(1)}, u32[]{:S(2)}, u32[]{:S(2)}) collective-permute-start(bf16[784,128]{1,0:T(8,128)(2,1)} %prepare_other.1), channel_id=1, source_target_pairs={{0,32},{32,0},{1,33},{33,1},{2,34},{34,2},{3,35},{35,3},{4,36},{36... | collective-permute-start | bytes 602120 | tf_op jit(solution)/shard_map/ppermute | solution.py:161
  5.7 3.1 %prepare_own.1 = (bf16[8,2,784,128]{3,2,1,0:T(8,128)(2,1)}, s16[1,384,128]{2,1,0:T(8,128)(2,1)}) custom-call(s32[1]{0:T(128)} %bitcast.1.low_ref, bf16[4,3,128,128]{3,2,1,0:T(8,128)(2,1)} %bitcast.14, s32[1,3,1,4]{3,2,1,0:T(1,128)} %bitcast.19, s32[3,8,32]{2,1,0:T(8,128)} %bitcast.17, s32[1,1,1,32]{3,2,1,0:T(1,128)} %counts.3, ...), custom_call_target="tpu_custom_call" | custom-call | flops 10000000 | bytes 4000000 | tf_op jit(solution)/shard_map/prepare_own/pallas_call | solution.py:162
  8.8 2.0 %collective-permute-done.other = bf16[784,128]{1,0:T(8,128)(2,1)S(1)} collective-permute-done((bf16[784,128]{1,0:T(8,128)(2,1)}, bf16[784,128]{1,0:T(8,128)(2,1)S(1)}, u32[]{:S(2)}, u32[]{:S(2)}) %collective-permute-start) | collective-permute-done | bytes 200736 | tf_op jit(solution)/shard_map/ppermute | solution.py:161
  10.9 1.3 %add_other.1 = bf16[8,2,784,128]{3,2,1,0:T(8,128)(2,1)} custom-call(s32[1]{0:T(128)} %bitcast.1.low_ref, bf16[784,128]{1,0:T(8,128)(2,1)S(1)} %collective-permute-done.other, bf16[8,2,784,128]{3,2,1,0:T(8,128)(2,1)} %get-tuple-element.14._), custom_call_target="tpu_custom_call", output_to_operand_aliasing={{}: (2, {})} | custom-call | tf_op jit(solution)/shard_map/add_other/pallas_call | solution.py:172
  12.1 0.0 copy-start.2
  12.1 4.4 %all-to-all-start = ((bf16[8,2,784,128]{3,2,1,0:T(8,128)(2,1)}), bf16[8,2,784,128]{3,2,1,0:T(8,128)(2,1)S(1)}, u32[]{:S(2)}, u32[]{:S(2)}) async-start(bf16[8,2,784,128]{3,2,1,0:T(8,128)(2,1)} %add_other.1), calls=%async_computation | async-start | bytes 6422528 | tf_op jit(solution)/shard_map/all_to_all | solution.py:182
  16.6 0.0 copy-done.2
  16.6 75.4 %all-gather.1.code_ref = s16[16,384,128]{2,1,0:T(8,128)(2,1)} all-gather(s16[1,384,128]{2,1,0:T(8,128)(2,1)S(1)} %copy-done.2), channel_id=1, replica_groups=mesh['row_high'=16,'row_low'=2,'col'=8,'layer'=4] {'row_high'}, dimensions={0}, use_global_device_ids=true | all-gather | bytes 1671168 | tf_op jit(solution)/shard_map/all_gather | solution.py:183
  92.0 0.0 all-to-all-done.b_ref
  92.0 0.0 copy-start
  92.0 1.4 %copy-done = s16[16,384,128]{2,1,0:T(8,128)(2,1)S(1)} copy-done((s16[16,384,128]{2,1,0:T(8,128)(2,1)S(1)}, s16[16,384,128]{2,1,0:T(8,128)(2,1)}, u32[]{:S(2)}) %copy-start) | copy-done | bytes 1572888
  93.4 2.8 %products.1 = f32[4,2,128,128]{3,2,1,0:T(8,128)S(1)} custom-call(s32[1]{0:T(128)} %bitcast.col_ref, s16[16,384,128]{2,1,0:T(8,128)(2,1)S(1)} %copy-done, bf16[8,2,784,128]{3,2,1,0:T(8,128)(2,1)S(1)} %all-to-all-done.b_ref), custom_call_target="tpu_custom_call" | custom-call | tf_op jit(solution)/shard_map/products/pallas_call | solution.py:184
  96.2 0.0 copy-start.1
  96.2 0.8 copy-done.1
  97.0 4.7 %all-to-all-start.1 = ((f32[8,128,128]{2,1,0:T(8,128)}), f32[8,128,128]{2,1,0:T(8,128)S(1)}, u32[]{:S(2)}, u32[]{:S(2)}) async-start(f32[8,128,128]{2,1,0:T(8,128)} %bitcast.12), calls=%async_computation.1 | async-start | bytes 1048576 | tf_op jit(solution)/shard_map/all_to_all | solution.py:192
  102.3 5.7 %all-to-all-done.1 = f32[8,128,128]{2,1,0:T(8,128)S(1)} async-done(((f32[8,128,128]{2,1,0:T(8,128)}), f32[8,128,128]{2,1,0:T(8,128)S(1)}, u32[]{:S(2)}, u32[]{:S(2)}) %all-to-all-start.1) | async-done | bytes 524320 | tf_op jit(solution)/shard_map/all_to_all | solution.py:192
  108.0 0.6 fusion
  (1 shorter events, 0.0 us)
Async XLA Ops:
  1.9 9.0 %collective-permute-start = (bf16[784,128]{1,0:T(8,128)(2,1)}, bf16[784,128]{1,0:T(8,128)(2,1)S(1)}, u32[]{:S(2)}, u32[]{:S(2)}) collective-permute-start(bf16[784,128]{1,0:T(8,128)(2,1)} %prepare_other.1), channel_id=1, source_target_pairs={{0,32},{32,0},{1,33},{33,1},{2,34},{34,2},{3,35},{35,3},{4,36},{36... | collective-permute-start | bytes 602120 | tf_op jit(solution)/shard_map/ppermute | solution.py:161
  12.1 4.5 %copy-start.2 = (s16[1,384,128]{2,1,0:T(8,128)(2,1)S(1)}, s16[1,384,128]{2,1,0:T(8,128)(2,1)}, u32[]{:S(2)}) copy-start(s16[1,384,128]{2,1,0:T(8,128)(2,1)} %get-tuple-element.12) | copy-start | bytes 294916
  12.1 79.9 %all-to-all-start = ((bf16[8,2,784,128]{3,2,1,0:T(8,128)(2,1)}), bf16[8,2,784,128]{3,2,1,0:T(8,128)(2,1)S(1)}, u32[]{:S(2)}, u32[]{:S(2)}) async-start(bf16[8,2,784,128]{3,2,1,0:T(8,128)(2,1)} %add_other.1), calls=%async_computation | async-start | bytes 6422528 | tf_op jit(solution)/shard_map/all_to_all | solution.py:182
  92.0 1.4 %copy-start = (s16[16,384,128]{2,1,0:T(8,128)(2,1)S(1)}, s16[16,384,128]{2,1,0:T(8,128)(2,1)}, u32[]{:S(2)}) copy-start(s16[16,384,128]{2,1,0:T(8,128)(2,1)} %all-gather.1.code_ref) | copy-start | bytes 4718596
  96.2 0.8 copy-start.1
  97.0 11.0 %all-to-all-start.1 = ((f32[8,128,128]{2,1,0:T(8,128)}), f32[8,128,128]{2,1,0:T(8,128)S(1)}, u32[]{:S(2)}, u32[]{:S(2)}) async-start(f32[8,128,128]{2,1,0:T(8,128)} %bitcast.12), calls=%async_computation.1 | async-start | bytes 1048576 | tf_op jit(solution)/shard_map/all_to_all | solution.py:192

commit v3 on v2

--- a/solution.py
+++ b/solution.py
@@ -89,13 +89,20 @@
         copy.wait()
 
 
-def products(col_ref, code_ref, b_ref, out_ref):
+def products(col_ref, code_hbm, b_ref, out_ref, code_ref, sems):
     n_cols = b_ref.shape[0]
+    first = pltpu.make_async_copy(code_hbm.at[:4], code_ref.at[:4], sems.at[0])
+    rest = pltpu.make_async_copy(code_hbm.at[4:], code_ref.at[4:], sems.at[1])
+    first.start()
+    rest.start()
     out_ref[...] = jnp.zeros_like(out_ref)
     lanes = lax.broadcasted_iota(jnp.int32, (W_ROWS, TILE), 1)
     weights = [b_ref[col_ref[0], q, 2 * PANEL :].astype(jnp.float32) for q in range(2)]
 
+    first.wait()
     for g in range(n_cols):
+        if g == 2:
+            rest.wait()
         chosen = [
             [
                 jnp.sum(jnp.where(lanes == 2 * (2 * g + at), weights[q], 0.0), axis=1, keepdims=True)
@@ -183,12 +190,17 @@
     left_all = lax.all_gather(codes, "row_high", axis=0, tiled=True)
     partial = pl.pallas_call(
         products,
-        out_shape=jax.ShapeDtypeStruct((4, 2, TILE, TILE), jnp.float32),
-        in_specs=[smem, vmem, vmem],
+        out_shape=pltpu.HBM((4, 2, TILE, TILE), jnp.float32),
+        in_specs=[smem, hbm, vmem],
         out_specs=vmem,
+        scratch_shapes=[pltpu.VMEM(left_all.shape, jnp.int16), pltpu.SemaphoreType.DMA((2,))],
         compiler_params=pltpu.CompilerParams(vmem_limit_bytes=16 * 1024 * 1024),
         name="products",
-    )(lax.axis_index("col").reshape(1), left_all, right_all)
+    )(
+        lax.axis_index("col").reshape(1),
+        pltpu.with_memory_space_constraint(left_all, pltpu.HBM),
+        pltpu.with_memory_space_constraint(right_all, pltpu.VMEM),
+    )
     shares = lax.all_to_all(
         partial.reshape(8, TILE, TILE), ("layer", "row_low"), 0, 0, tiled=True
     )

time: 110 us -> 108 us (0.982)
  local copies, waits for them, and re-layouts: 2.2 us -> 0.01 us
  Pallas kernels: 9.02 us -> 11 us
  blocking collectives: 75.4 us -> 74 us
    unnamed x6 -> x2, local copies, waits for them, and re-layouts: 2.2 us -> 0.01 us
    pallas_call x1, Pallas kernels: 2.77 us -> 4.74 us  [local(): pl.pallas_call(products, out_shape=pltpu.HBM((4, 2, TILE, TILE), jnp.floa...]
    all_gather x1, blocking collectives: 75.4 us -> 74 us  [local(): left_all = lax.all_gather(codes, 'row_high', axis=0, tiled=True)]
where the time goes in v3:
time: 108 us; the launch traced here: 107 us
  blocking collectives  74 us (69%)
  starting transfers between devices  13 us (12%)
  Pallas kernels  11 us (10%)
  waiting for transfers between devices  7.67 us (7%)
    all_gather x1, blocking collectives, local(): left_all = lax.all_gather(codes, 'row_high', axis=0, tiled=True)  74 us
    all_to_all x1, waiting for transfers between devices, local(): lax.all_to_all(partial.reshape(8, TILE, TILE), ('layer', 'row_low'), 0, 0...  5.66 us
    pallas_call x1, Pallas kernels, local(): pl.pallas_call(products, out_shape=pltpu.HBM((4, 2, TILE, TILE), jnp.floa...  4.74 us
    all_to_all x1, starting transfers between devices, local(): lax.all_to_all(partial.reshape(8, TILE, TILE), ('layer', 'row_low'), 0, 0...  4.7 us
    all_to_all x1, starting transfers between devices, local(): right_all = lax.all_to_all(right, 'col', 0, 0, tiled=True)  4.44 us
    ppermute x1, starting transfers between devices, local(): other = lax.ppermute(send, 'row_low', [(0, 1), (1, 0)])  3.81 us
    pallas_call x1, Pallas kernels, local(): pl.pallas_call(prepare_own, out_shape=(spread, jax.ShapeDtypeStruct((1, P...  3.16 us
  transfers between devices with their start and end apart: 3, of which 2 were waited for; matrix products, arithmetic and copies ran while one was open for 0% of the time, Pallas kernels for 3%

profile of v3, /device:TPU:24, one launch (start us, length us, event | category | flops | bytes accessed | tf_op | source)
XLA Modules:
  0.0 107.0 jit_solution(6291500950095377433)
XLA Ops:
  0.0 1.9 %prepare_other.1 = bf16[784,128]{1,0:T(8,128)(2,1)} custom-call(s32[1]{0:T(128)} %bitcast.1.low_ref, bf16[4,3,128,128]{3,2,1,0:T(8,128)(2,1)} %bitcast.13, s32[1,3,1,4]{3,2,1,0:T(1,128)} %bitcast.18, s32[3,8,32]{2,1,0:T(8,128)} %bitcast.16, s32[1,1,1,32]{3,2,1,0:T(1,128)} %counts.3), custom_call_target="tpu_custom_call" | custom-call | tf_op jit(solution)/shard_map/prepare_other/pallas_call | solution.py:161
  1.9 3.8 %collective-permute-start = (bf16[784,128]{1,0:T(8,128)(2,1)}, bf16[784,128]{1,0:T(8,128)(2,1)S(1)}, u32[]{:S(2)}, u32[]{:S(2)}) collective-permute-start(bf16[784,128]{1,0:T(8,128)(2,1)} %prepare_other.1), channel_id=1, source_target_pairs={{0,32},{32,0},{1,33},{33,1},{2,34},{34,2},{3,35},{35,3},{4,36},{36... | collective-permute-start | bytes 602120 | tf_op jit(solution)/shard_map/ppermute | solution.py:168
  5.7 3.2 %prepare_own.1 = (bf16[8,2,784,128]{3,2,1,0:T(8,128)(2,1)}, s16[1,384,128]{2,1,0:T(8,128)(2,1)}) custom-call(s32[1]{0:T(128)} %bitcast.1.low_ref, bf16[4,3,128,128]{3,2,1,0:T(8,128)(2,1)} %bitcast.14, s32[1,3,1,4]{3,2,1,0:T(1,128)} %bitcast.19, s32[3,8,32]{2,1,0:T(8,128)} %bitcast.17, s32[1,1,1,32]{3,2,1,0:T(1,128)} %counts.3, ...), custom_call_target="tpu_custom_call" | custom-call | flops 10000000 | bytes 4000000 | tf_op jit(solution)/shard_map/prepare_own/pallas_call | solution.py:169
  8.9 2.0 %collective-permute-done.other = bf16[784,128]{1,0:T(8,128)(2,1)S(1)} collective-permute-done((bf16[784,128]{1,0:T(8,128)(2,1)}, bf16[784,128]{1,0:T(8,128)(2,1)S(1)}, u32[]{:S(2)}, u32[]{:S(2)}) %collective-permute-start) | collective-permute-done | bytes 200736 | tf_op jit(solution)/shard_map/ppermute | solution.py:168
  10.9 1.2 %add_other.1 = bf16[8,2,784,128]{3,2,1,0:T(8,128)(2,1)} custom-call(s32[1]{0:T(128)} %bitcast.1.low_ref, bf16[784,128]{1,0:T(8,128)(2,1)S(1)} %collective-permute-done.other, bf16[8,2,784,128]{3,2,1,0:T(8,128)(2,1)} %get-tuple-element.14._), custom_call_target="tpu_custom_call", output_to_operand_aliasing={{}: (2, {})} | custom-call | tf_op jit(solution)/shard_map/add_other/pallas_call | solution.py:179
  12.1 0.0 copy-start
  12.1 4.4 %all-to-all-start = ((bf16[8,2,784,128]{3,2,1,0:T(8,128)(2,1)}), bf16[8,2,784,128]{3,2,1,0:T(8,128)(2,1)S(1)}, u32[]{:S(2)}, u32[]{:S(2)}) async-start(bf16[8,2,784,128]{3,2,1,0:T(8,128)(2,1)} %add_other.1), calls=%async_computation | async-start | bytes 6422528 | tf_op jit(solution)/shard_map/all_to_all | solution.py:189
  16.6 0.0 copy-done
  16.6 74.0 %all-gather.1.code_hbm = s16[16,384,128]{2,1,0:T(8,128)(2,1)} all-gather(s16[1,384,128]{2,1,0:T(8,128)(2,1)S(1)} %copy-done), channel_id=1, replica_groups=mesh['row_high'=16,'row_low'=2,'col'=8,'layer'=4] {'row_high'}, dimensions={0}, use_global_device_ids=true | all-gather | bytes 1671168 | tf_op jit(solution)/shard_map/all_gather | solution.py:190
  90.5 0.0 all-to-all-done.b_ref
  90.5 4.7 %products.1 = f32[4,2,128,128]{3,2,1,0:T(8,128)} custom-call(s32[1]{0:T(128)} %bitcast.col_ref, s16[16,384,128]{2,1,0:T(8,128)(2,1)} %all-gather.1.code_hbm, bf16[8,2,784,128]{3,2,1,0:T(8,128)(2,1)S(1)} %all-to-all-done.b_ref), custom_call_target="tpu_custom_call" | custom-call | tf_op jit(solution)/shard_map/products/pallas_call | solution.py:191
  95.3 4.7 %all-to-all-start.1 = ((f32[8,128,128]{2,1,0:T(8,128)}), f32[8,128,128]{2,1,0:T(8,128)S(1)}, u32[]{:S(2)}, u32[]{:S(2)}) async-start(f32[8,128,128]{2,1,0:T(8,128)} %bitcast.12), calls=%async_computation.1 | async-start | bytes 1048576 | tf_op jit(solution)/shard_map/all_to_all | solution.py:204
  100.7 5.7 %all-to-all-done.1 = f32[8,128,128]{2,1,0:T(8,128)S(1)} async-done(((f32[8,128,128]{2,1,0:T(8,128)}), f32[8,128,128]{2,1,0:T(8,128)S(1)}, u32[]{:S(2)}, u32[]{:S(2)}) %all-to-all-start.1) | async-done | bytes 524320 | tf_op jit(solution)/shard_map/all_to_all | solution.py:204
  106.3 0.6 fusion
  (1 shorter events, 0.0 us)
Async XLA Ops:
  1.9 9.0 %collective-permute-start = (bf16[784,128]{1,0:T(8,128)(2,1)}, bf16[784,128]{1,0:T(8,128)(2,1)S(1)}, u32[]{:S(2)}, u32[]{:S(2)}) collective-permute-start(bf16[784,128]{1,0:T(8,128)(2,1)} %prepare_other.1), channel_id=1, source_target_pairs={{0,32},{32,0},{1,33},{33,1},{2,34},{34,2},{3,35},{35,3},{4,36},{36... | collective-permute-start | bytes 602120 | tf_op jit(solution)/shard_map/ppermute | solution.py:168
  12.1 4.5 %copy-start = (s16[1,384,128]{2,1,0:T(8,128)(2,1)S(1)}, s16[1,384,128]{2,1,0:T(8,128)(2,1)}, u32[]{:S(2)}) copy-start(s16[1,384,128]{2,1,0:T(8,128)(2,1)} %get-tuple-element.12) | copy-start | bytes 294916
  12.1 78.4 %all-to-all-start = ((bf16[8,2,784,128]{3,2,1,0:T(8,128)(2,1)}), bf16[8,2,784,128]{3,2,1,0:T(8,128)(2,1)S(1)}, u32[]{:S(2)}, u32[]{:S(2)}) async-start(bf16[8,2,784,128]{3,2,1,0:T(8,128)(2,1)} %add_other.1), calls=%async_computation | async-start | bytes 6422528 | tf_op jit(solution)/shard_map/all_to_all | solution.py:189
  95.3 11.0 %all-to-all-start.1 = ((f32[8,128,128]{2,1,0:T(8,128)}), f32[8,128,128]{2,1,0:T(8,128)S(1)}, u32[]{:S(2)}, u32[]{:S(2)}) async-start(f32[8,128,128]{2,1,0:T(8,128)} %bitcast.12), calls=%async_computation.1 | async-start | bytes 1048576 | tf_op jit(solution)/shard_map/all_to_all | solution.py:204

commit v4 on v3

--- a/solution.py
+++ b/solution.py
@@ -32,13 +32,23 @@
     return ((scaled - 4.0 * exponent) * jnp.exp2(exponent - 61.0)).astype(jnp.bfloat16)
 
 
-def right_block(low, parity, b_ref, b_occ, block):
+def fetch_panels(parity, b_hbm, tiles, sems):
+    copies = [
+        pltpu.make_async_copy(b_hbm.at[2 * half + parity], tiles.at[half], sems.at[half])
+        for half in range(2)
+    ]
+    for copy in copies:
+        copy.start()
+    return copies
+
+
+def right_block(parity, tiles, b_occ, block):
     for half in range(2):
         for t in range(RIGHT):
             row = half * PANEL + t * TILE
-            panel = 2 * half + parity
-            tile = b_ref[panel, t]
-            block[row : row + TILE] = jnp.where(b_occ[0, t, 0, panel] > 0, tile, jnp.zeros_like(tile))
+            tile = tiles[half, t]
+            held = b_occ[0, t, 0, 2 * half + parity] > 0
+            block[row : row + TILE] = jnp.where(held, tile, jnp.zeros_like(tile))
 
 
 def stack_weights(stacks, counts):
@@ -66,17 +76,25 @@
     return copies
 
 
-def prepare_other(low_ref, b_ref, b_occ, stacks, counts, send_ref):
-    low = low_ref[0]
-    put_weights(1 - low, stack_weights(stacks, counts), send_ref)
-    right_block(low, 1 - low, b_ref, b_occ, send_ref)
-
-
-def prepare_own(low_ref, b_ref, b_occ, stacks, counts, a_ref, a_occ, out_ref, code_ref, own, sems):
-    low = low_ref[0]
-    put_weights(low, stack_weights(stacks, counts), own)
-    right_block(low, low, b_ref, b_occ, own)
-    copies = copy_all(own, out_ref, low, sems)
+def prepare_other(low_ref, b_hbm, b_occ, stacks, counts, send_ref, tiles, sems):
+    parity = 1 - low_ref[0]
+    copies = fetch_panels(parity, b_hbm, tiles, sems)
+    put_weights(parity, stack_weights(stacks, counts), send_ref)
+    for copy in copies:
+        copy.wait()
+    right_block(parity, tiles, b_occ, send_ref)
+
+
+def prepare_own(
+    low_ref, b_hbm, b_occ, stacks, counts, a_ref, a_occ, out_ref, code_ref, own, tiles, sems, out_sems
+):
+    parity = low_ref[0]
+    copies = fetch_panels(parity, b_hbm, tiles, sems)
+    put_weights(parity, stack_weights(stacks, counts), own)
+    for copy in copies:
+        copy.wait()
+    right_block(parity, tiles, b_occ, own)
+    copies = copy_all(own, out_ref, parity, out_sems)
     for s in range(LEFT):
         held = a_ref[s].astype(jnp.float32) * a_occ[0, 0, 0, s].astype(jnp.float32)
         code_ref[0, s * TILE : (s + 1) * TILE] = encode(held)
@@ -91,29 +109,31 @@
 
 def products(col_ref, code_hbm, b_ref, out_ref, code_ref, sems):
     n_cols = b_ref.shape[0]
-    first = pltpu.make_async_copy(code_hbm.at[:4], code_ref.at[:4], sems.at[0])
-    rest = pltpu.make_async_copy(code_hbm.at[4:], code_ref.at[4:], sems.at[1])
-    first.start()
-    rest.start()
+    copies = [
+        pltpu.make_async_copy(code_hbm.at[pl.ds(2 * at, 2)], code_ref.at[pl.ds(2 * at, 2)], sems.at[at])
+        for at in range(n_cols)
+    ]
+    for copy in copies:
+        copy.start()
     out_ref[...] = jnp.zeros_like(out_ref)
     lanes = lax.broadcasted_iota(jnp.int32, (W_ROWS, TILE), 1)
     weights = [b_ref[col_ref[0], q, 2 * PANEL :].astype(jnp.float32) for q in range(2)]
-
-    first.wait()
+    chosen = [
+        [
+            jnp.sum(jnp.where(lanes == 2 * panel, weights[q], 0.0), axis=1, keepdims=True)
+            for q in range(2)
+        ]
+        for panel in range(2 * n_cols)
+    ]
+
+    copies[0].wait()
     for g in range(n_cols):
-        if g == 2:
-            rest.wait()
-        chosen = [
-            [
-                jnp.sum(jnp.where(lanes == 2 * (2 * g + at), weights[q], 0.0), axis=1, keepdims=True)
-                for q in range(2)
-            ]
-            for at in range(2)
-        ]
-
+        if g == 1:
+            for copy in copies[1:]:
+                copy.wait()
         def weighted(at, q, s, t):
             number = s * RIGHT + t
-            weight = jnp.broadcast_to(chosen[at][q][number : number + 1], (16, TILE)).astype(jnp.bfloat16)
+            weight = jnp.broadcast_to(chosen[2 * g + at][q][number : number + 1], (16, TILE)).astype(jnp.bfloat16)
             row = at * PANEL + t * TILE
             tile = b_ref[g, q, row : row + TILE]
             return (tile.reshape(8, 16, TILE) * weight[None]).reshape(TILE, TILE)
@@ -151,30 +171,41 @@
     smem = pl.BlockSpec(memory_space=pltpu.SMEM)
     hbm = pl.BlockSpec(memory_space=pltpu.HBM)
     low = lax.axis_index("row_low").reshape(1)
-    spread = jax.ShapeDtypeStruct((n_cols, 2, BLOCK, TILE), jnp.bfloat16)
+    in_hbm = lambda array: pltpu.with_memory_space_constraint(array, pltpu.HBM)
+    in_vmem = lambda array: pltpu.with_memory_space_constraint(array, pltpu.VMEM)
+    params = pltpu.CompilerParams(vmem_limit_bytes=16 * 1024 * 1024)
+    spread = pltpu.HBM((n_cols, 2, BLOCK, TILE), jnp.bfloat16)
+    panels = [pltpu.VMEM((2, RIGHT, TILE, TILE), jnp.bfloat16), pltpu.SemaphoreType.DMA((2,))]
     right_args = (
-        b_tiles[:, 0, 0],
-        b_occ.transpose(1, 3, 2, 0),
-        stacks[0, 0, 0].transpose(2, 1, 0),
-        stack_count,
+        in_hbm(b_tiles[:, 0, 0]),
+        in_hbm(b_occ.transpose(1, 3, 2, 0)),
+        in_hbm(stacks[0, 0, 0].transpose(2, 1, 0)),
+        in_hbm(stack_count),
     )
     send = pl.pallas_call(
         prepare_other,
-        out_shape=jax.ShapeDtypeStruct((BLOCK, TILE), jnp.bfloat16),
-        in_specs=[smem, vmem, smem, vmem, vmem],
+        out_shape=pltpu.VMEM((BLOCK, TILE), jnp.bfloat16),
+        in_specs=[smem, hbm, smem, vmem, vmem],
         out_specs=vmem,
+        scratch_shapes=panels,
+        compiler_params=params,
         name="prepare_other",
     )(low, *right_args)
     other = lax.ppermute(send, "row_low", [(0, 1), (1, 0)])
     right, codes = pl.pallas_call(
         prepare_own,
-        out_shape=(spread, jax.ShapeDtypeStruct((1, PANEL, TILE), jnp.int16)),
-        in_specs=[smem, vmem, smem, vmem, vmem, vmem, smem],
+        out_shape=(spread, pltpu.HBM((1, PANEL, TILE), jnp.int16)),
+        in_specs=[smem, hbm, smem, vmem, vmem, vmem, smem],
         out_specs=(hbm, vmem),
-        scratch_shapes=[pltpu.VMEM((BLOCK, TILE), jnp.bfloat16), pltpu.SemaphoreType.DMA((n_cols,))],
+        scratch_shapes=[
+            pltpu.VMEM((BLOCK, TILE), jnp.bfloat16),
+            *panels,
+            pltpu.SemaphoreType.DMA((n_cols,)),
+        ],
+        compiler_params=params,
         cost_estimate=pl.CostEstimate(flops=10_000_000, bytes_accessed=4_000_000, transcendentals=0),
         name="prepare_own",
-    )(low, *right_args, a_tiles[0, 0, 0], a_occ)
+    )(low, *right_args, in_hbm(a_tiles[0, 0, 0]), in_hbm(a_occ))
     other, right, codes = lax.optimization_barrier((other, right, codes))
     right = pl.pallas_call(
         add_other,
@@ -183,9 +214,9 @@
         out_specs=hbm,
         scratch_shapes=[pltpu.SemaphoreType.DMA((n_cols,))],
         input_output_aliases={2: 0},
-        compiler_params=pltpu.CompilerParams(vmem_limit_bytes=54_000_000),
+        compiler_params=params,
         name="add_other",
-    )(low, other, right)
+    )(low, in_vmem(other), in_hbm(right))
     right_all = lax.all_to_all(right, "col", 0, 0, tiled=True)
     left_all = lax.all_gather(codes, "row_high", axis=0, tiled=True)
     partial = pl.pallas_call(
@@ -193,13 +224,13 @@
         out_shape=pltpu.HBM((4, 2, TILE, TILE), jnp.float32),
         in_specs=[smem, hbm, vmem],
         out_specs=vmem,
-        scratch_shapes=[pltpu.VMEM(left_all.shape, jnp.int16), pltpu.SemaphoreType.DMA((2,))],
-        compiler_params=pltpu.CompilerParams(vmem_limit_bytes=16 * 1024 * 1024),
+        scratch_shapes=[pltpu.VMEM(left_all.shape, jnp.int16), pltpu.SemaphoreType.DMA((n_cols,))],
+        compiler_params=params,
         name="products",
     )(
         lax.axis_index("col").reshape(1),
-        pltpu.with_memory_space_constraint(left_all, pltpu.HBM),
-        pltpu.with_memory_space_constraint(right_all, pltpu.VMEM),
+        in_hbm(left_all),
+        in_vmem(right_all),
     )
     shares = lax.all_to_all(
         partial.reshape(8, TILE, TILE), ("layer", "row_low"), 0, 0, tiled=True

time: 108 us -> 108 us (level)
  transfers between devices with their start and end apart: 3 -> 3, of which waited for: 2 -> 2; matrix products, arithmetic and copies ran while one was open for 0% -> 0% of each run, Pallas kernels for 3% -> 4%
where the time goes in v4:
time: 108 us; the launch traced here: 107 us
  blocking collectives  73.9 us (68%)
  starting transfers between devices  13 us (12%)
  Pallas kernels  11.5 us (11%)
  waiting for transfers between devices  6.76 us (6%)
    all_gather x1, blocking collectives, local(): left_all = lax.all_gather(codes, 'row_high', axis=0, tiled=True)  73.9 us
    all_to_all x1, waiting for transfers between devices, local(): lax.all_to_all(partial.reshape(8, TILE, TILE), ('layer', 'row_low'), 0, 0...  5.66 us
    all_to_all x1, starting transfers between devices, local(): lax.all_to_all(partial.reshape(8, TILE, TILE), ('layer', 'row_low'), 0, 0...  4.78 us
    pallas_call x1, Pallas kernels, local(): pl.pallas_call(products, out_shape=pltpu.HBM((4, 2, TILE, TILE), jnp.floa...  4.71 us
    all_to_all x1, starting transfers between devices, local(): right_all = lax.all_to_all(right, 'col', 0, 0, tiled=True)  4.44 us
    pallas_call x1, Pallas kernels, local(): pl.pallas_call(prepare_own, out_shape=(spread, pltpu.HBM((1, PANEL, TILE)...  3.86 us
    ppermute x1, starting transfers between devices, local(): other = lax.ppermute(send, 'row_low', [(0, 1), (1, 0)])  3.83 us
  transfers between devices with their start and end apart: 3, of which 2 were waited for; matrix products, arithmetic and copies ran while one was open for 0% of the time, Pallas kernels for 4%

profile of v4, /device:TPU:24, one launch (start us, length us, event | category | flops | bytes accessed | tf_op | source)
XLA Modules:
  0.0 106.6 jit_solution(15143976466412786024)
XLA Ops:
  0.0 1.7 %prepare_other.1 = bf16[784,128]{1,0:T(8,128)(2,1)S(1)} custom-call(s32[1]{0:T(128)} %bitcast.1.low_ref, bf16[4,3,128,128]{3,2,1,0:T(8,128)(2,1)} %bitcast.13, s32[1,3,1,4]{3,2,1,0:T(1,128)} %bitcast.18, s32[3,8,32]{2,1,0:T(8,128)} %bitcast.16, s32[1,1,1,32]{3,2,1,0:T(1,128)} %counts.3), custom_call_target="tpu_custom_call" | custom-call | tf_op jit(solution)/shard_map/prepare_other/pallas_call | solution.py:185
  1.7 3.8 %collective-permute-start = (bf16[784,128]{1,0:T(8,128)(2,1)S(1)}, bf16[784,128]{1,0:T(8,128)(2,1)S(1)}, u32[]{:S(2)}, u32[]{:S(2)}) collective-permute-start(bf16[784,128]{1,0:T(8,128)(2,1)S(1)} %prepare_other.1), channel_id=1, source_target_pairs={{0,32},{32,0},{1,33},{33,1},{2,34},{34,2},{3,35},{35,3},{4,36},{36... | collective-permute-start | bytes 602120 | tf_op jit(solution)/shard_map/ppermute | solution.py:194
  5.6 3.9 %prepare_own.1 = (bf16[8,2,784,128]{3,2,1,0:T(8,128)(2,1)}, s16[1,384,128]{2,1,0:T(8,128)(2,1)}) custom-call(s32[1]{0:T(128)} %bitcast.1.low_ref, bf16[4,3,128,128]{3,2,1,0:T(8,128)(2,1)} %bitcast.14, s32[1,3,1,4]{3,2,1,0:T(1,128)} %bitcast.19, s32[3,8,32]{2,1,0:T(8,128)} %bitcast.17, s32[1,1,1,32]{3,2,1,0:T(1,128)} %counts.3, ...), custom_call_target="tpu_custom_call" | custom-call | flops 10000000 | bytes 4000000 | tf_op jit(solution)/shard_map/prepare_own/pallas_call | solution.py:195
  9.4 1.1 %collective-permute-done.other = bf16[784,128]{1,0:T(8,128)(2,1)S(1)} collective-permute-done((bf16[784,128]{1,0:T(8,128)(2,1)S(1)}, bf16[784,128]{1,0:T(8,128)(2,1)S(1)}, u32[]{:S(2)}, u32[]{:S(2)}) %collective-permute-start) | collective-permute-done | bytes 200736 | tf_op jit(solution)/shard_map/ppermute | solution.py:194
  10.5 1.2 %add_other.1 = bf16[8,2,784,128]{3,2,1,0:T(8,128)(2,1)} custom-call(s32[1]{0:T(128)} %bitcast.1.low_ref, bf16[784,128]{1,0:T(8,128)(2,1)S(1)} %collective-permute-done.other, bf16[8,2,784,128]{3,2,1,0:T(8,128)(2,1)} %get-tuple-element.14._), custom_call_target="tpu_custom_call", output_to_operand_aliasing={{}: (2, {})} | custom-call | tf_op jit(solution)/shard_map/add_other/pallas_call | solution.py:210
  11.8 0.0 copy-start
  11.8 4.4 %all-to-all-start = ((bf16[8,2,784,128]{3,2,1,0:T(8,128)(2,1)}), bf16[8,2,784,128]{3,2,1,0:T(8,128)(2,1)S(1)}, u32[]{:S(2)}, u32[]{:S(2)}) async-start(bf16[8,2,784,128]{3,2,1,0:T(8,128)(2,1)} %add_other.1), calls=%async_computation | async-start | bytes 6422528 | tf_op jit(solution)/shard_map/all_to_all | solution.py:220
  16.2 0.0 copy-done
  16.2 73.9 %all-gather.1.code_hbm = s16[16,384,128]{2,1,0:T(8,128)(2,1)} all-gather(s16[1,384,128]{2,1,0:T(8,128)(2,1)S(1)} %copy-done), channel_id=1, replica_groups=mesh['row_high'=16,'row_low'=2,'col'=8,'layer'=4] {'row_high'}, dimensions={0}, use_global_device_ids=true | all-gather | bytes 1671168 | tf_op jit(solution)/shard_map/all_gather | solution.py:221
  90.1 0.0 all-to-all-done.b_ref
  90.1 4.7 %products.1 = f32[4,2,128,128]{3,2,1,0:T(8,128)} custom-call(s32[1]{0:T(128)} %bitcast.col_ref, s16[16,384,128]{2,1,0:T(8,128)(2,1)} %all-gather.1.code_hbm, bf16[8,2,784,128]{3,2,1,0:T(8,128)(2,1)S(1)} %all-to-all-done.b_ref), custom_call_target="tpu_custom_call" | custom-call | tf_op jit(solution)/shard_map/products/pallas_call | solution.py:222
  94.9 4.8 %all-to-all-start.1 = ((f32[8,128,128]{2,1,0:T(8,128)}), f32[8,128,128]{2,1,0:T(8,128)S(1)}, u32[]{:S(2)}, u32[]{:S(2)}) async-start(f32[8,128,128]{2,1,0:T(8,128)} %bitcast.12), calls=%async_computation.1 | async-start | bytes 1048576 | tf_op jit(solution)/shard_map/all_to_all | solution.py:235
  100.3 5.7 %all-to-all-done.1 = f32[8,128,128]{2,1,0:T(8,128)S(1)} async-done(((f32[8,128,128]{2,1,0:T(8,128)}), f32[8,128,128]{2,1,0:T(8,128)S(1)}, u32[]{:S(2)}, u32[]{:S(2)}) %all-to-all-start.1) | async-done | bytes 524320 | tf_op jit(solution)/shard_map/all_to_all | solution.py:235
  106.0 0.6 fusion
  (1 shorter events, 0.0 us)
Async XLA Ops:
  1.7 8.8 %collective-permute-start = (bf16[784,128]{1,0:T(8,128)(2,1)S(1)}, bf16[784,128]{1,0:T(8,128)(2,1)S(1)}, u32[]{:S(2)}, u32[]{:S(2)}) collective-permute-start(bf16[784,128]{1,0:T(8,128)(2,1)S(1)} %prepare_other.1), channel_id=1, source_target_pairs={{0,32},{32,0},{1,33},{33,1},{2,34},{34,2},{3,35},{35,3},{4,36},{36... | collective-permute-start | bytes 602120 | tf_op jit(solution)/shard_map/ppermute | solution.py:194
  11.8 4.5 %copy-start = (s16[1,384,128]{2,1,0:T(8,128)(2,1)S(1)}, s16[1,384,128]{2,1,0:T(8,128)(2,1)}, u32[]{:S(2)}) copy-start(s16[1,384,128]{2,1,0:T(8,128)(2,1)} %get-tuple-element.12) | copy-start | bytes 294916
  11.8 78.4 %all-to-all-start = ((bf16[8,2,784,128]{3,2,1,0:T(8,128)(2,1)}), bf16[8,2,784,128]{3,2,1,0:T(8,128)(2,1)S(1)}, u32[]{:S(2)}, u32[]{:S(2)}) async-start(bf16[8,2,784,128]{3,2,1,0:T(8,128)(2,1)} %add_other.1), calls=%async_computation | async-start | bytes 6422528 | tf_op jit(solution)/shard_map/all_to_all | solution.py:220
  94.9 11.1 %all-to-all-start.1 = ((f32[8,128,128]{2,1,0:T(8,128)}), f32[8,128,128]{2,1,0:T(8,128)S(1)}, u32[]{:S(2)}, u32[]{:S(2)}) async-start(f32[8,128,128]{2,1,0:T(8,128)} %bitcast.12), calls=%async_computation.1 | async-start | bytes 1048576 | tf_op jit(solution)/shard_map/all_to_all | solution.py:235
